TPU v7x, 32 devices: a whole 2x2x4 slice. The times are simulated.
32 devices in a mesh: row: 8 (over z, core), col: 4 (over y, x).
Axes of the slice: x: 2, y: 2, z: 4, core: 2. Of those that a mesh axis runs over, the one named last changes fastest.
Arguments:
- gram: float32 [9, 512, 8, 2048], P(None, 'row', None, 'col'), may hold values from 0 to 4, as said below
Outputs:
- trailing: float32 [9, 512, 8, 2048], P(None, 'row', None, 'col')
- factor: float32 [8, 4, 512, 512], P(None, 'col', 'row')
Inputs may be any that keep to these rules, and one draw needn't show every extreme that they name: gram holds the first 4608 rows of a symmetric positive definite 16384 x 16384 matrix whose smallest eigenvalue is at least 0.5.
All inputs are finite; a program needn't handle non-finite values.
Results may differ from a plain program's by a relative error of at most 0.0003.
Values sent between devices are 32-bit elements; how exact they have to be, the bound alone decides.
No kernel may reach another device: no remote copies, remote signals or barrier semaphores. Data moves between devices by JAX's collectives and lax.ppermute only.
A program may use at most 64 MiB of HBM per device.

v0:
```python
import functools

import jax
import jax.numpy as jnp
from jax import lax
from jax.experimental import pallas as pl
from jax.experimental.pallas import tpu as pltpu
from jax.sharding import PartitionSpec as P

HIGHEST = lax.Precision.HIGHEST
SUBLANES = 8
LANES = 128
VMEM = pl.BlockSpec(memory_space=pltpu.VMEM)
ANY = pl.BlockSpec(memory_space=pl.ANY)
HBM = pl.BlockSpec(memory_space=pltpu.HBM)
SMEM = pl.BlockSpec(memory_space=pltpu.SMEM)


def f32(*shape):
    return jax.ShapeDtypeStruct(shape, jnp.float32)


def bf16(*shape):
    return jax.ShapeDtypeStruct(shape, jnp.bfloat16)


def call(kernel, out_shape, in_specs, out_specs, scratch=(), limit=16 << 20, aliases=None, micros=1):
    n_in, n_out = len(in_specs), len(out_specs)

    def with_token(_, *refs):
        refs[n_in + n_out][...] = jnp.zeros((SUBLANES, LANES), jnp.float32)
        kernel(*refs[: n_in + n_out], *refs[n_in + n_out + 1 :])

    return pl.pallas_call(
        with_token,
        out_shape=[*out_shape, f32(SUBLANES, LANES)],
        in_specs=[ANY, *in_specs],
        out_specs=[*out_specs, VMEM],
        scratch_shapes=list(scratch),
        input_output_aliases={i + 1: o for i, o in (aliases or {}).items()},
        cost_estimate=pl.CostEstimate(flops=int(micros * 5 * 10**7), bytes_accessed=0, transcendentals=0),
        compiler_params=pltpu.CompilerParams(vmem_limit_bytes=limit),
    )


def split(value):
    high = value.astype(jnp.bfloat16)
    return high, (value - high.astype(jnp.float32)).astype(jnp.bfloat16)


def dot3(a, b, dims=(((1,), (0,)), ((), ()))):
    dot = lambda x, y: lax.dot_general(x, y, dims, preferred_element_type=jnp.float32)
    return dot(a[0], b[0]) + (dot(a[0], b[1]) + dot(a[1], b[0]))


def prepare_kernel(order, held, chunks, diagonal):
    diagonal[...] = held[:, 0, :]
    for i, q in enumerate(order):
        for c in range(held.shape[1]):
            chunks[i, c] = held[:, c, q * LANES : (q + 1) * LANES]


def prepare(token, tile_row, order):
    part_rows, col_tiles, tile = tile_row.shape
    return call(
        functools.partial(prepare_kernel, order),
        [f32(len(order), col_tiles, part_rows, LANES), f32(part_rows, tile)],
        [VMEM],
        [VMEM] * 2,
        limit=8 << 20,
    )(token, tile_row)


def panel_kernel(place, gram, panel, held, sems):
    count = panel.shape[0]
    keep = place[2] == 0
    copies = [pltpu.make_async_copy(gram.at[a + 1], held.at[a % 4], sems.at[a % 4]) for a in range(count)]
    for a in range(min(4, count)):
        copies[a].start()
    for a in range(count):
        copies[a].wait()
        panel[a] = jnp.where(keep, held[a % 4, :, 0, :], 0.0)
        if a + 4 < count:
            copies[a + 4].start()


def take_panel(token, place, gram):
    slab, part_rows, col_tiles, tile = gram.shape
    return call(
        panel_kernel,
        [f32(slab - 1, part_rows, tile)],
        [SMEM, HBM],
        [VMEM],
        [pltpu.VMEM((4, part_rows, col_tiles, tile), jnp.float32), pltpu.SemaphoreType.DMA((4,))],
        limit=52 << 20,
        micros=4,
    )(token, place, gram)


def factor_block(groups):
    shape = (SUBLANES, LANES)
    sub = lax.broadcasted_iota(jnp.int32, shape, 0)
    lane = lax.broadcasted_iota(jnp.int32, shape, 1)
    row = lambda v, j: jnp.broadcast_to(v[j : j + 1, :], shape)
    col = lambda v, l: jnp.broadcast_to(v[:, l : l + 1], shape)
    groups = list(groups)
    upper, inverse = [], []
    for b in range(len(groups)):
        lo = SUBLANES * b
        panel = (lane >= lo) & (lane < lo + SUBLANES)
        rows_u = groups[b]
        rows_z = jnp.where(panel, jnp.where(lane == sub + lo, 1.0, 0.0), rows_u)
        columns = [col(rows_u, lo + j) for j in range(SUBLANES)]
        u_out, w_out, pivots = rows_u, rows_z, jnp.ones(shape, jnp.float32)
        for j in range(SUBLANES):
            pivot = row(columns[j], j)
            recip = 1.0 / pivot
            here = sub == j
            mult = jnp.where(here, 1.0 - recip, columns[j] * recip)
            z_row, u_row = row(rows_z, j), row(rows_u, j)
            u_out = jnp.where(here, u_row, u_out)
            w_out = jnp.where(here, z_row, w_out)
            pivots = jnp.where(here, pivot, pivots)
            for m in range(j + 1, SUBLANES):
                columns[m] = columns[m] - mult * row(columns[m], j)
            rows_z = rows_z - mult * z_row
            rows_u = rows_u - mult * u_row
        scale = lax.rsqrt(pivots)
        upper.append(jnp.where(lane >= lo + sub, u_out * scale, 0.0))
        inverse.append(jnp.where(lane <= lo + sub, w_out * scale, 0.0))
        z_rows = [row(rows_z, j) for j in range(SUBLANES)]
        for i in range(b + 1, len(groups)):
            g = groups[i]
            even = col(g, lo) * z_rows[0]
            odd = col(g, lo + 1) * z_rows[1]
            for j in range(2, SUBLANES, 2):
                even = even + col(g, lo + j) * z_rows[j]
                odd = odd + col(g, lo + j + 1) * z_rows[j + 1]
            groups[i] = jnp.where(panel, 0.0, g) - (even + odd)
    return upper, inverse


def block_step(p, n_blocks, state, u_ref):
    offset = pl.multiple_of(p * LANES, LANES)
    block = pl.ds(offset, LANES)
    groups = LANES // SUBLANES
    rows8 = [pl.ds(pl.multiple_of(offset + SUBLANES * i, SUBLANES), SUBLANES) for i in range(groups)]
    upper, inverse = factor_block([state[r, block] for r in rows8])
    for i in range(groups):
        u_ref[rows8[i], block] = upper[i]
        state[rows8[i], block] = inverse[i]
    own_inverse = state[block, block]

    def row_panel(i, _):
        at = pl.ds(pl.multiple_of(i * LANES, LANES), LANES)
        old = jnp.where(i == p, jnp.eye(LANES, dtype=jnp.float32), state[block, at])
        state[block, at] = jnp.dot(own_inverse, old, precision=HIGHEST, preferred_element_type=jnp.float32)
        return 0

    lax.fori_loop(0, n_blocks, row_panel, 0)

    def below(i, _):
        at = pl.ds(pl.multiple_of(i * LANES, LANES), LANES)
        coupling = state[block, at]
        u_ref[block, at] = coupling
        state[at, block] = jnp.zeros((LANES, LANES), jnp.float32)
        change = lax.dot_general(
            coupling, state[block, :], (((0,), (0,)), ((), ())), precision=HIGHEST, preferred_element_type=jnp.float32
        )
        state[at, :] = state[at, :] - change
        return 0

    lax.fori_loop(p + 1, n_blocks, below, 0)


def cholesky_kernel(first, last, n_own, n_z, place, *refs):
    if first == 0:
        own, other = refs[:n_own], refs[n_own : 2 * n_own]
        state, u_ref, sems = refs[2 * n_own :]
        z, core, c = place[0], place[1], place[2]
        rows = own[0].shape[0] // n_z
        copies = []
        for k, half in ((core, own), (1 - core, other)):
            for m, part in enumerate(half):
                for s in range(n_z):
                    zz = lax.rem(z - s + n_z, n_z)
                    at = ((zz * 2 + k) * n_own + lax.bitwise_xor(c, m)) * rows
                    copies.append(
                        pltpu.make_async_copy(
                            part.at[pl.ds(s * rows, rows), :],
                            state.at[pl.ds(pl.multiple_of(at, rows), rows), :],
                            sems.at[len(copies)],
                        )
                    )
        for copy in copies:
            copy.start()
        for copy in copies:
            copy.wait()
        u_ref[...] = jnp.zeros_like(u_ref)
    else:
        state_in, u_in, state, u_ref = refs
        state[...] = state_in[...]
        u_ref[...] = u_in[...]
    n_blocks = state.shape[0] // LANES

    def step(p, _):
        block_step(p, n_blocks, state, u_ref)
        return 0

    lax.fori_loop(first, last, step, 0)


def cholesky_start(token, place, own, other, tile, last, n_z):
    return call(
        functools.partial(cholesky_kernel, 0, last, len(own), n_z),
        [f32(tile, tile)] * 2,
        [SMEM] + [ANY] * (2 * len(own)),
        [VMEM] * 2,
        [pltpu.SemaphoreType.DMA((2 * len(own) * n_z,))],
        limit=8 << 20,
        micros=60,
    )(token, place, *own, *other)


def cholesky_next(token, place, state, first, last):
    return call(
        functools.partial(cholesky_kernel, first, last, 0, 0),
        [f32(*state[0].shape)] * 2,
        [SMEM, VMEM, VMEM],
        [VMEM] * 2,
        limit=8 << 20,
        micros=20,
    )(token, place, *state)


def weights_kernel(place, state, u_ref, *refs):
    n_parts = len(refs) - 6
    parts = refs[:n_parts]
    x_high, x_low, w_high, w_low, own_l, lower = refs[n_parts:]
    tile = state.shape[0]
    z, core, c = place[0], place[1], place[2]
    r = lax.broadcasted_iota(jnp.int32, (tile, tile), 0)
    s = lax.broadcasted_iota(jnp.int32, (tile, tile), 1)
    w = jnp.where(s <= r, state[...], 0.0)
    w_parts = split(w)
    w_high[...], w_low[...] = split(w.T)
    panel = jnp.concatenate([parts[i][...] + parts[i + 1][...] for i in range(0, n_parts, 2)], 0)
    g = dot3(split(panel), w_parts, (((1,), (1,)), ((), ())))
    x_high[...], x_low[...] = split(dot3(split(g), w_parts))
    part_rows = own_l.shape[0]
    lower[...] = u_ref[...].T
    own_l[...] = lower[pl.ds(pl.multiple_of((z * 2 + core) * part_rows, part_rows), part_rows), :]


def weights(token, place, state, upper, parts, part_rows):
    tile = state.shape[0]
    total = sum(part.shape[0] for part in parts) // 2
    return call(
        weights_kernel,
        [bf16(total, tile)] * 2 + [bf16(tile, tile)] * 2 + [f32(part_rows, tile)],
        [SMEM] + [VMEM] * (2 + len(parts)),
        [VMEM] * 5,
        [pltpu.VMEM((tile, tile), jnp.float32)],
    )(token, place, state, upper, *parts)


def own_columns(row0, fac, at, part_rows):
    col_tiles, depth = row0.shape[0], row0.shape[1]
    for t in range(col_tiles):
        fac[t, :, 0:depth] = row0[t].T
    return fac[:, pl.ds(at, part_rows), 0:depth].reshape(col_tiles * part_rows, depth)


def update_kernel(chunks, starts, n_hops, place, gram, x_high, x_low, w_high, w_low, own_l, *refs):
    sources, rest = refs[: 1 + 2 * n_hops], refs[1 + 2 * n_hops :]
    trailing, factor, row0, old, new, zero, fac, prod, block_sems, old_sems, new_sems, zero_sems, fac_sem = rest[-13:]
    z, core, c = place[0], place[1], place[2]
    n_z = n_hops + 1
    _, cores, col_tiles, part_rows, lanes = sources[0].shape
    count, tile = old.shape[1], row0.shape[2]
    first_col = c == 0
    x = (x_high[...], x_low[...])

    def transfers(i):
        position, q = chunks[i]
        slot, here = i % 2, pl.ds(q * lanes, lanes)
        jobs = [(None, 0, z)]
        for s in range(1, n_hops + 1):
            for below, zz, inside in ((0, z - s, z >= s), (1, z + s, z + s < n_z)):
                jobs.append((inside & (core == below), s, zz))
                jobs.append((inside & (core != below), n_hops + s, zz))
        found = [(None, pltpu.make_async_copy(gram.at[pl.ds(1, count), :, :, here], old.at[slot], old_sems.at[slot]))]
        for job, (condition, source, zz) in enumerate(jobs):
            for k in range(cores):
                at = pl.multiple_of((zz * cores + k) * part_rows, part_rows)
                origin = sources[source].at[position - starts[source], k]
                target = row0.at[slot, :, pl.ds(at, part_rows), :]
                found.append((condition, pltpu.make_async_copy(origin, target, block_sems.at[slot, job, k])))
        return found

    def each(i, action):
        for condition, copy in transfers(i):
            if condition is None:
                action(copy)
            else:
                pl.when(condition)(functools.partial(action, copy))

    each(0, lambda copy: copy.start())
    zero[...] = jnp.zeros(zero.shape, jnp.float32)
    zeros = [
        pltpu.make_async_copy(zero, trailing.at[0, :, :, pl.ds(q * lanes, lanes)], zero_sems.at[i])
        for i, (_, q) in enumerate(chunks)
    ]
    outs = []
    mine = (z * cores + core) * part_rows
    place_factor = pltpu.make_async_copy(fac.at[:, pl.ds(0, part_rows), :], factor.at[:, 0], fac_sem)
    owner = [mine // lanes == q for _, q in chunks]
    for i, (_, q) in enumerate(chunks):
        slot, here = i % 2, pl.ds(q * lanes, lanes)
        if i + 1 < len(chunks):
            each(i + 1, lambda copy: copy.start())
        each(i, lambda copy: copy.wait())
        if i == 0:
            for copy in zeros:
                copy.start()
        if i >= 2:
            outs[i - 2].wait()
        for t in range(0, col_tiles, 2):
            column = split(jnp.concatenate([row0[slot, t], row0[slot, t + 1]], axis=1))
            product = dot3(x, column)
            prod[t] = product[:, :LANES]
            prod[t + 1] = product[:, LANES:]
        sub = lax.broadcasted_iota(jnp.int32, (part_rows, col_tiles, LANES), 1)
        for a in range(count):
            part = jnp.swapaxes(prod[:, a * part_rows : (a + 1) * part_rows, :], 0, 1)
            new[slot, a] = jnp.where(first_col & (sub == 0), 0.0, old[slot, a] - part)
        outs.append(
            pltpu.make_async_copy(new.at[slot], trailing.at[pl.ds(1, count), :, :, here], new_sems.at[slot])
        )
        outs[i].start()

        @pl.when(owner[i])
        def _():
            at = pl.multiple_of(mine % lanes, part_rows)
            across = own_columns(row0.at[slot], fac, at, part_rows)
            value = dot3(split(across), (w_high[...], w_low[...])).reshape(col_tiles, part_rows, tile)
            fac[:, 0:part_rows, :] = value
            fac[0, 0:part_rows, :] = jnp.where(first_col, own_l[...], value[0])
            place_factor.start()

    for is_owner in owner:
        pl.when(is_owner)(place_factor.wait)
    for copy in outs[-2:] + zeros:
        copy.wait()


def update(token, chunks, place, gram, weight, sources, previous):
    slab, part_rows, col_tiles, tile = gram.shape
    n_hops = (len(sources) - 1) // 2
    count = slab - 1
    operands = [place, gram, *weight, *(array for array, _ in sources)]
    specs = [SMEM, HBM] + [VMEM] * 5 + [ANY] * len(sources)
    aliases = {}
    if previous is not None:
        aliases = {len(operands): 0, len(operands) + 1: 1}
        operands += list(previous)
        specs += [HBM] * 2
    slots = pltpu.VMEM((2, count, part_rows, col_tiles, LANES), jnp.float32)
    scratch = [
        pltpu.VMEM((2, col_tiles, tile, LANES), jnp.float32),
        slots,
        slots,
        pltpu.VMEM((part_rows, col_tiles, LANES), jnp.float32),
        pltpu.VMEM((col_tiles, LANES, tile), jnp.float32),
        pltpu.VMEM((col_tiles, count * part_rows, LANES), jnp.float32),
        pltpu.SemaphoreType.DMA((2, 1 + 4 * n_hops, 2)),
        pltpu.SemaphoreType.DMA((2,)),
        pltpu.SemaphoreType.DMA((2,)),
        pltpu.SemaphoreType.DMA((len(chunks),)),
        pltpu.SemaphoreType.DMA,
    ]
    return call(
        functools.partial(update_kernel, chunks, [start for _, start in sources], n_hops),
        [f32(*gram.shape), f32(col_tiles, 1, part_rows, tile)],
        specs,
        [HBM, HBM],
        scratch,
        limit=26 << 20,
        micros=0,
        aliases=aliases,
    )(token, *operands)


def scatter(parts, root, axis):
    here = lax.axis_index(axis) == root
    mine = jnp.where(here, parts[0], 0.0)
    sent = [lax.ppermute(part, axis, [(root, i)]) for i, part in enumerate(parts) if i != root]
    return functools.reduce(jnp.add, sent, mine)


def exchange(part, axis, size):
    return [part] + [lax.ppermute(part, axis, [(i, i ^ m) for i in range(size)]) for m in range(1, size)]


def together(*values):
    return lax.optimization_barrier(values)


def body(gram, rows, cols):
    slab, part_rows, col_tiles, tile = gram.shape
    n_z = rows // 2
    n_chunks = tile // LANES
    n_blocks = tile // LANES
    core = lax.axis_index("row") % 2
    place = jnp.stack([lax.axis_index("row") // 2, core, lax.axis_index("col")]).astype(jnp.int32)
    other_core = [(i, i ^ 1) for i in range(rows)]
    swap = lambda value: lax.ppermute(value, "row", other_core)
    spread = lambda value, level: lax.ppermute(value, "col", [(i, i + level) for i in range(level)])

    def hop(value, s):
        pairs = [(2 * z, 2 * z + 2) for z in range(s - 1, n_z - 1)]
        pairs += [(2 * z + 1, 2 * z - 1) for z in range(1, n_z - s + 1)]
        return lax.ppermute(value, "row", pairs)

    order = sorted(range(n_chunks), key=lambda q: -abs(2 * q - n_chunks + 1))
    token = jnp.zeros((SUBLANES, LANES), jnp.float32)
    chunks, diagonal, token = prepare(token, gram[0], order)
    share = part_rows // cols
    piece = scatter([diagonal[i * share : (i + 1) * share] for i in range(cols)], 0, "col")
    partner = swap(chunks)
    blocks = jnp.stack([jnp.where(core == 0, chunks, partner), jnp.where(core == 0, partner, chunks)], 1)

    piece, blocks, token = together(piece, blocks, token)
    ring = [piece]
    for s in range(1, n_z):
        ring.append(lax.ppermute(piece, "row", [(i, (i + 2 * s) % rows) for i in range(rows)]))
    piece = jnp.concatenate(ring, 0)
    panel, token = take_panel(token, place, gram)
    panel = panel.reshape((slab - 1) * part_rows, tile)
    levels = cols.bit_length() - 1
    piece, blocks, token = together(piece, blocks, token)
    hops = [hop(blocks, 1)]
    halves = exchange(piece, "col", cols)
    panel, *halves = together(panel, *halves)
    others = [swap(half) for half in halves]

    height = panel.shape[0]
    bounds = [0, height * 2 // 5 // SUBLANES * SUBLANES, height * 7 // 10 // SUBLANES * SUBLANES, height]
    held = [panel[first:last] for first, last in zip(bounds[:-1], bounds[1:])]
    sent = [None] * len(held)

    def launch(step):
        moving = [i for i in range(len(held)) if 0 <= step - i < levels]
        for i in moving:
            if step > i:
                held[i] = held[i] + sent[i]
            sent[i] = spread(held[i], 1 << (step - i))
        return moving

    for p in range(n_blocks):
        moving = launch(p)
        if p == 0:
            *state, token = cholesky_start(token, place, halves, others, tile, 1, n_z)
        else:
            if p == n_blocks - 1:
                token, *hops = together(token, *hops)
            *state, token = cholesky_next(token, place, state, p, p + 1)
        if p == 0:
            token, hops[0], sent[0] = together(token, hops[0], sent[0])
            for s in range(2, n_z - 1):
                hops.append(hop(hops[-1], s))
        else:
            token, *landed = together(token, *(sent[i] for i in moving))
            for i, value in zip(moving, landed):
                sent[i] = value
    for step in range(n_blocks, len(held) + levels - 1):
        launch(step)
    parts = [value for pair in zip(held, sent) for value in pair]
    swapped = [swap(value) for value in hops]

    pair = n_chunks // 2
    finals = [hop(hops[-1][i : i + pair], n_z - 1) for i in (0, pair)]
    *weight, token = weights(token, place, *state, parts, part_rows)
    outs = None
    for final, first in zip(finals, (0, pair)):
        token, final = together(token, final)
        sources = [(value, 0) for value in (blocks, *hops)] + [(final, first)]
        sources += [(value, 0) for value in swapped] + [(swap(final), first)]
        positions = [(i, order[i]) for i in range(first, first + pair)]
        *outs, token = update(token, positions, place, gram, weight, sources, outs)
    return tuple(outs)


def solution(mesh):
    rows, cols = mesh.shape["row"], mesh.shape["col"]
    return jax.shard_map(
        functools.partial(body, rows=rows, cols=cols),
        mesh=mesh,
        in_specs=(P(None, "row", None, "col"),),
        out_specs=(P(None, "row", None, "col"), P(None, "col", "row", None)),
        check_vma=False,
    )
```

profile of v0, /device:TPU:21, one launch (start us, length us, event | category | flops | bytes accessed | tf_op | source)
XLA Modules:
  0.0 121.2 jit_solution(5079253244682543007)
XLA Ops:
  0.6 1.3 %slice_bitcast_fusion.refs_0_ = f32[64,8,512]{2,1,0:T(8,128)S(1)} fusion(f32[9,64,8,512]{3,2,1,0:T(8,128)} %refs_1_.5), kind=kLoop, calls=%fused_computation.3 | loop fusion | bytes 2097152 | tf_op jit(solution)/shard_map/squeeze | solution.py:427
  4.6 1.3 %collective-permute-start.1 = (f32[16,512]{1,0:T(8,128)S(1)}, f32[16,512]{1,0:T(8,128)S(1)}, u32[]{:S(2)}, u32[]{:S(2)}) collective-permute-start(f32[16,512]{1,0:T(8,128)S(1)} %get-tuple-element.122), channel_id=1, source_target_pairs={{0,2},{4,6},{8,10},{12,14},{16,18},{20,22},{24,26},{28,30}} | collective-permute-start | bytes 98312 | tf_op jit(solution)/shard_map/ppermute | solution.py:397
  6.0 4.9 %collective-permute-done.1 = f32[16,512]{1,0:T(8,128)S(1)} collective-permute-done((f32[16,512]{1,0:T(8,128)S(1)}, f32[16,512]{1,0:T(8,128)S(1)}, u32[]{:S(2)}, u32[]{:S(2)}) %collective-permute-start.1) | collective-permute-done | bytes 32800 | tf_op jit(solution)/shard_map/ppermute | solution.py:397
  11.5 3.2 %collective-permute-start.5 = (f32[16,512]{1,0:T(8,128)S(1)}, f32[16,512]{1,0:T(8,128)S(1)}, u32[]{:S(2)}, u32[]{:S(2)}) collective-permute-start(f32[16,512]{1,0:T(8,128)S(1)} %add_add_fusion), channel_id=1, source_target_pairs={{0,16},{4,20},{8,24},{12,28},{16,0},{20,4},{24,8},{28,12},{1,17},{... | collective-permute-start | bytes 98312 | tf_op jit(solution)/shard_map/ppermute | solution.py:436
  14.8 4.2 %shard_map.31 = (f32[8,64,512]{2,1,0:T(8,128)S(1)}, f32[8,128]{1,0:T(8,128)S(1)}) custom-call(f32[8,128]{1,0:T(8,128)S(1)} %get-tuple-element.64._, s32[3]{0:T(128)S(1)} %pad_add_fusion.refs_0_, f32[9,64,8,512]{3,2,1,0:T(8,128)} %refs_1_.5), custom_call_target="tpu_custom_call" | custom-call | flops 200000000 | tf_op jit(solution)/shard_map/pallas_call | solution.py:89
  19.1 3.4 %collective-permute-start.14 = (f32[4,2,8,64,128]{4,3,2,1,0:T(8,128)S(1)}, f32[4,2,8,64,128]{4,3,2,1,0:T(8,128)S(1)}, u32[]{:S(2)}, u32[]{:S(2)}) collective-permute-start(f32[4,2,8,64,128]{4,3,2,1,0:T(8,128)S(1)} %pad_maximum_fusion.refs_7_), channel_id=1, source_target_pairs={{0,8},{8,16},{16,24},{12,4},{20,12},{28,20},{1,9},{9,17},{17,25},{... | collective-permute-start | bytes 6291464 | tf_op jit(solution)/shard_map/ppermute | solution.py:423
  22.6 1.1 collective-permute-start.8
  23.6 1.6 %collective-permute-start.7 = (f32[64,512]{1,0:T(8,128)S(1)}, f32[64,512]{1,0:T(8,128)S(1)}, u32[]{:S(2)}, u32[]{:S(2)}) collective-permute-start(f32[64,512]{1,0:T(8,128)S(1)} %pad_maximum_fusion.1.refs_1_), channel_id=1, source_target_pairs={{0,1},{1,0},{2,3},{3,2},{4,5},{5,4},{6,7},{7,6},{8,9},{9,8},{10,11... | collective-permute-start | bytes 393224 | tf_op jit(solution)/shard_map/ppermute | solution.py:402
  25.2 2.2 %collective-permute-done.9.refs_4_ = f32[64,512]{1,0:T(8,128)S(1)} collective-permute-done((f32[64,512]{1,0:T(8,128)S(1)}, f32[64,512]{1,0:T(8,128)S(1)}, u32[]{:S(2)}, u32[]{:S(2)}) %collective-permute-start.9) | collective-permute-done | bytes 131104 | tf_op jit(solution)/shard_map/ppermute | solution.py:402
  27.4 1.3 %collective-permute-done.8.refs_3_ = f32[64,512]{1,0:T(8,128)S(1)} collective-permute-done((f32[64,512]{1,0:T(8,128)S(1)}, f32[64,512]{1,0:T(8,128)S(1)}, u32[]{:S(2)}, u32[]{:S(2)}) %collective-permute-start.8) | collective-permute-done | bytes 131104 | tf_op jit(solution)/shard_map/ppermute | solution.py:402
  29.1 2.3 %collective-permute-start.10 = (f32[64,512]{1,0:T(8,128)S(1)}, f32[64,512]{1,0:T(8,128)S(1)}, u32[]{:S(2)}, u32[]{:S(2)}) collective-permute-start(f32[64,512]{1,0:T(8,128)S(1)} %pad_maximum_fusion.1.refs_1_), channel_id=1, source_target_pairs={{0,4},{4,0},{8,12},{12,8},{16,20},{20,16},{24,28},{28,24},{1,5},{5... | collective-permute-start | bytes 393224 | tf_op jit(solution)/shard_map/ppermute | solution.py:417
  33.2 9.1 %shard_map.32 = (f32[512,512]{1,0:T(8,128)S(1)}, f32[512,512]{1,0:T(8,128)S(1)}, f32[8,128]{1,0:T(8,128)S(1)}) custom-call(f32[8,128]{1,0:T(8,128)S(1)} %get-tuple-element.66._, s32[3]{0:T(128)S(1)} %pad_add_fusion.refs_0_, f32[64,512]{1,0:T(8,128)S(1)} %pad_maximum_fusion.1.refs_1_, f32[64,512]{1,0:T(8,128)S(1)} %collective-permute-done.7.refs_2_, ...), custom_call_target="tpu_custom_call" | custom-call | flops 3000000000 | tf_op jit(solution)/shard_map/pallas_call | solution.py:214
  42.4 3.8 %collective-permute-done.14.refs_8_ = f32[4,2,8,64,128]{4,3,2,1,0:T(8,128)S(1)} collective-permute-done((f32[4,2,8,64,128]{4,3,2,1,0:T(8,128)S(1)}, f32[4,2,8,64,128]{4,3,2,1,0:T(8,128)S(1)}, u32[]{:S(2)}, u32[]{:S(2)}) %collective-permute-start.14) | collective-permute-done | bytes 2097184 | tf_op jit(solution)/shard_map/ppermute | solution.py:423
  46.2 3.5 %collective-permute-start.20 = (f32[4,2,8,64,128]{4,3,2,1,0:T(8,128)S(1)}, f32[4,2,8,64,128]{4,3,2,1,0:T(8,128)S(1)}, u32[]{:S(2)}, u32[]{:S(2)}) collective-permute-start(f32[4,2,8,64,128]{4,3,2,1,0:T(8,128)S(1)} %collective-permute-done.14.refs_8_), channel_id=1, source_target_pairs={{8,16},{16,24},{12,4},{20,12},{9,17},{17,25},{13,5},{21,13},{10,18... | collective-permute-start | bytes 6291464 | tf_op jit(solution)/shard_map/ppermute | solution.py:423
  49.7 1.3 %collective-permute-start.16 = (f32[200,512]{1,0:T(8,128)S(1)}, f32[200,512]{1,0:T(8,128)S(1)}, u32[]{:S(2)}, u32[]{:S(2)}) collective-permute-start(f32[200,512]{1,0:T(8,128)S(1)} %slice_add_fusion.2.refs_3_), channel_id=1, source_target_pairs={{0,2},{1,3},{4,6},{5,7},{8,10},{9,11},{12,14},{13,15},{16,18},{17,... | collective-permute-start | bytes 1228808 | tf_op jit(solution)/shard_map/ppermute | solution.py:418
  52.5 6.7 %shard_map.33 = (f32[512,512]{1,0:T(8,128)S(1)}, f32[512,512]{1,0:T(8,128)S(1)}, f32[8,128]{1,0:T(8,128)S(1)}) custom-call(f32[8,128]{1,0:T(8,128)S(1)} %get-tuple-element.76._, s32[3]{0:T(128)S(1)} %pad_add_fusion.refs_0_, f32[512,512]{1,0:T(8,128)S(1)} %get-tuple-element.77.refs_1_, f32[512,512]{1,0:T(8,128)S(1)} %get-tuple-element.78.refs_2_), custom_call_target="tpu_custom_call" | custom-call | flops 1000000000 | tf_op jit(solution)/shard_map/pallas_call | solution.py:226
  59.2 0.9 collective-permute-done.16.refs_4_
  60.2 1.5 %collective-permute-start.18 = (f32[152,512]{1,0:T(8,128)S(1)}, f32[152,512]{1,0:T(8,128)S(1)}, u32[]{:S(2)}, u32[]{:S(2)}) collective-permute-start(f32[152,512]{1,0:T(8,128)S(1)} %slice_add_fusion.refs_5_), channel_id=1, source_target_pairs={{0,2},{1,3},{4,6},{5,7},{8,10},{9,11},{12,14},{13,15},{16,18},{17,... | collective-permute-start | bytes 933896 | tf_op jit(solution)/shard_map/ppermute | solution.py:418
  61.7 6.3 %shard_map.34 = (f32[512,512]{1,0:T(8,128)S(1)}, f32[512,512]{1,0:T(8,128)S(1)}, f32[8,128]{1,0:T(8,128)S(1)}) custom-call(f32[8,128]{1,0:T(8,128)S(1)} %get-tuple-element.81._, s32[3]{0:T(128)S(1)} %pad_add_fusion.refs_0_, f32[512,512]{1,0:T(8,128)S(1)} %get-tuple-element.82.refs_1_, f32[512,512]{1,0:T(8,128)S(1)} %get-tuple-element.83.refs_2_), custom_call_target="tpu_custom_call" | custom-call | flops 1000000000 | tf_op jit(solution)/shard_map/pallas_call | solution.py:226
  68.0 1.1 collective-permute-done.18.refs_6_
  69.0 3.5 %collective-permute-done.20.refs_9_ = f32[4,2,8,64,128]{4,3,2,1,0:T(8,128)S(1)} collective-permute-done((f32[4,2,8,64,128]{4,3,2,1,0:T(8,128)S(1)}, f32[4,2,8,64,128]{4,3,2,1,0:T(8,128)S(1)}, u32[]{:S(2)}, u32[]{:S(2)}) %collective-permute-start.20) | collective-permute-done | bytes 2097184 | tf_op jit(solution)/shard_map/ppermute | solution.py:423
  73.4 7.0 %collective-permute-start.23 = (f32[4,2,8,64,128]{4,3,2,1,0:T(8,128)S(1)}, f32[4,2,8,64,128]{4,3,2,1,0:T(8,128)S(1)}, u32[]{:S(2)}, u32[]{:S(2)}) collective-permute-start(f32[4,2,8,64,128]{4,3,2,1,0:T(8,128)S(1)} %collective-permute-done.14.refs_8_), channel_id=1, source_target_pairs={{0,4},{4,0},{8,12},{12,8},{16,20},{20,16},{24,28},{28,24},{1,5},{5... | collective-permute-start | bytes 6291464 | tf_op jit(solution)/shard_map/ppermute | solution.py:417
  80.5 1.3 %collective-permute-start.21 = (f32[160,512]{1,0:T(8,128)S(1)}, f32[160,512]{1,0:T(8,128)S(1)}, u32[]{:S(2)}, u32[]{:S(2)}) collective-permute-start(f32[160,512]{1,0:T(8,128)S(1)} %slice_add_fusion.1.refs_7_), channel_id=1, source_target_pairs={{0,2},{1,3},{4,6},{5,7},{8,10},{9,11},{12,14},{13,15},{16,18},{17,... | collective-permute-start | bytes 983048 | tf_op jit(solution)/shard_map/ppermute | solution.py:418
  81.8 5.8 %shard_map.35 = (f32[512,512]{1,0:T(8,128)S(1)}, f32[512,512]{1,0:T(8,128)S(1)}, f32[8,128]{1,0:T(8,128)S(1)}) custom-call(f32[8,128]{1,0:T(8,128)S(1)} %get-tuple-element.88._, s32[3]{0:T(128)S(1)} %pad_add_fusion.refs_0_, f32[512,512]{1,0:T(8,128)S(1)} %get-tuple-element.89.refs_1_, f32[512,512]{1,0:T(8,128)S(1)} %get-tuple-element.90.refs_2_), custom_call_target="tpu_custom_call" | custom-call | flops 1000000000 | tf_op jit(solution)/shard_map/pallas_call | solution.py:226
  87.7 3.6 %collective-permute-done.21.refs_8_ = f32[160,512]{1,0:T(8,128)S(1)} collective-permute-done((f32[160,512]{1,0:T(8,128)S(1)}, f32[160,512]{1,0:T(8,128)S(1)}, u32[]{:S(2)}, u32[]{:S(2)}) %collective-permute-start.21) | collective-permute-done | bytes 327712 | tf_op jit(solution)/shard_map/ppermute | solution.py:418
  91.3 2.4 %shard_map.36 = (bf16[512,512]{1,0:T(8,128)(2,1)S(1)}, bf16[512,512]{1,0:T(8,128)(2,1)S(1)}, bf16[512,512]{1,0:T(8,128)(2,1)S(1)}, bf16[512,512]{1,0:T(8,128)(2,...) custom-call(f32[8,128]{1,0:T(8,128)S(1)} %get-tuple-element.93._, s32[3]{0:T(128)S(1)} %pad_add_fusion.refs_0_, ...), custom_call_target="tpu_custom_call" | custom-call | flops 50000000 | tf_op jit(solution)/shard_map/pallas_call | solution.py:258
  93.7 1.3 %collective-permute-start.25 = (f32[2,2,8,64,128]{4,3,2,1,0:T(8,128)S(1)}, f32[2,2,8,64,128]{4,3,2,1,0:T(8,128)S(1)}, u32[]{:S(2)}, u32[]{:S(2)}) collective-permute-start(f32[2,2,8,64,128]{4,3,2,1,0:T(8,128)S(1)} %collective-permute-done.22.refs_10_), channel_id=1, source_target_pairs={{0,4},{4,0},{8,12},{12,8},{16,20},{20,16},{24,28},{28,24},{1,5},{5... | collective-permute-start | bytes 3145736 | tf_op jit(solution)/shard_map/ppermute | solution.py:417
  95.7 1.6 %collective-permute-done.25.refs_13_ = f32[2,2,8,64,128]{4,3,2,1,0:T(8,128)S(1)} collective-permute-done((f32[2,2,8,64,128]{4,3,2,1,0:T(8,128)S(1)}, f32[2,2,8,64,128]{4,3,2,1,0:T(8,128)S(1)}, u32[]{:S(2)}, u32[]{:S(2)}) %collective-permute-start.25) | collective-permute-done | bytes 1048608 | tf_op jit(solution)/shard_map/ppermute | solution.py:417
  97.3 8.0 %shard_map.37 = (f32[9,64,8,512]{3,2,1,0:T(8,128)}, f32[8,1,64,512]{3,2,1,0:T(8,128)}, f32[8,128]{1,0:T(8,128)S(1)}) custom-call(f32[8,128]{1,0:T(8,128)S(1)} %get-tuple-element.101._, s32[3]{0:T(128)S(1)} %pad_add_fusion.refs_0_, f32[9,64,8,512]{3,2,1,0:T(8,128)S(1)} %bitcast.13, bf16[512,512]{1,0:T(8,128)(2,1)S(1)} %get-tuple-element.102.refs_2_, ...), custom_call_target="tpu_custom_call" | custom-call | tf_op jit(solution)/shard_map/pallas_call | solution.py:382
  105.3 3.9 %collective-permute-start.27 = (f32[2,2,8,64,128]{4,3,2,1,0:T(8,128)S(1)}, f32[2,2,8,64,128]{4,3,2,1,0:T(8,128)S(1)}, u32[]{:S(2)}, u32[]{:S(2)}) collective-permute-start(f32[2,2,8,64,128]{4,3,2,1,0:T(8,128)S(1)} %collective-permute-done.26.refs_10_), channel_id=1, source_target_pairs={{0,4},{4,0},{8,12},{12,8},{16,20},{20,16},{24,28},{28,24},{1,5},{5... | collective-permute-start | bytes 3145736 | tf_op jit(solution)/shard_map/ppermute | solution.py:417
  109.2 2.3 %collective-permute-done.27.refs_13_ = f32[2,2,8,64,128]{4,3,2,1,0:T(8,128)S(1)} collective-permute-done((f32[2,2,8,64,128]{4,3,2,1,0:T(8,128)S(1)}, f32[2,2,8,64,128]{4,3,2,1,0:T(8,128)S(1)}, u32[]{:S(2)}, u32[]{:S(2)}) %collective-permute-start.27) | collective-permute-done | bytes 1048608 | tf_op jit(solution)/shard_map/ppermute | solution.py:417
  111.5 9.5 %shard_map.38 = (f32[9,64,8,512]{3,2,1,0:T(8,128)}, f32[8,1,64,512]{3,2,1,0:T(8,128)}, f32[8,128]{1,0:T(8,128)}) custom-call(f32[8,128]{1,0:T(8,128)S(1)} %get-tuple-element.110._, s32[3]{0:T(128)S(1)} %pad_add_fusion.refs_0_, f32[9,64,8,512]{3,2,1,0:T(8,128)S(1)} %bitcast.13, ...), custom_call_target="tpu_custom_call", output_to_operand_aliasing={{0}: (15, {}), {1}: (16, {})} | custom-call | tf_op jit(solution)/shard_map/pallas_call | solution.py:382
  (55 shorter events, 9.0 us)
Async XLA Ops:
  2.5 8.3 %collective-permute-start.3 = (f32[4,8,64,128]{3,2,1,0:T(8,128)S(1)}, f32[4,8,64,128]{3,2,1,0:T(8,128)S(1)}, u32[]{:S(2)}, u32[]{:S(2)}) collective-permute-start(f32[4,8,64,128]{3,2,1,0:T(8,128)S(1)} %get-tuple-element.60), channel_id=1, source_target_pairs={{0,4},{4,0},{8,12},{12,8},{16,20},{20,16},{24,28},{28,24},{1,5},{5... | collective-permute-start | bytes 3145736 | tf_op jit(solution)/shard_map/ppermute | solution.py:417
  3.3 2.7 %collective-permute-start = (f32[16,512]{1,0:T(8,128)S(1)}, f32[16,512]{1,0:T(8,128)S(1)}, u32[]{:S(2)}, u32[]{:S(2)}) collective-permute-start(f32[16,512]{1,0:T(8,128)S(1)} %get-tuple-element.120), channel_id=1, source_target_pairs={{0,1},{4,5},{8,9},{12,13},{16,17},{20,21},{24,25},{28,29}} | collective-permute-start | bytes 98312 | tf_op jit(solution)/shard_map/ppermute | solution.py:397
  3.9 2.0 %collective-permute-start.2 = (f32[16,512]{1,0:T(8,128)S(1)}, f32[16,512]{1,0:T(8,128)S(1)}, u32[]{:S(2)}, u32[]{:S(2)}) collective-permute-start(f32[16,512]{1,0:T(8,128)S(1)} %get-tuple-element.121), channel_id=1, source_target_pairs={{0,3},{4,7},{8,11},{12,15},{16,19},{20,23},{24,27},{28,31}} | collective-permute-start | bytes 98312 | tf_op jit(solution)/shard_map/ppermute | solution.py:397
  4.6 6.2 %collective-permute-start.1 = (f32[16,512]{1,0:T(8,128)S(1)}, f32[16,512]{1,0:T(8,128)S(1)}, u32[]{:S(2)}, u32[]{:S(2)}) collective-permute-start(f32[16,512]{1,0:T(8,128)S(1)} %get-tuple-element.122), channel_id=1, source_target_pairs={{0,2},{4,6},{8,10},{12,14},{16,18},{20,22},{24,26},{28,30}} | collective-permute-start | bytes 98312 | tf_op jit(solution)/shard_map/ppermute | solution.py:397
  11.3 7.8 %collective-permute-start.6 = (f32[16,512]{1,0:T(8,128)S(1)}, f32[16,512]{1,0:T(8,128)S(1)}, u32[]{:S(2)}, u32[]{:S(2)}) collective-permute-start(f32[16,512]{1,0:T(8,128)S(1)} %add_add_fusion), channel_id=1, source_target_pairs={{0,24},{4,28},{8,0},{12,4},{16,8},{20,12},{24,16},{28,20},{1,25},{... | collective-permute-start | bytes 98312 | tf_op jit(solution)/shard_map/ppermute | solution.py:436
  11.5 7.5 %collective-permute-start.5 = (f32[16,512]{1,0:T(8,128)S(1)}, f32[16,512]{1,0:T(8,128)S(1)}, u32[]{:S(2)}, u32[]{:S(2)}) collective-permute-start(f32[16,512]{1,0:T(8,128)S(1)} %add_add_fusion), channel_id=1, source_target_pairs={{0,16},{4,20},{8,24},{12,28},{16,0},{20,4},{24,8},{28,12},{1,17},{... | collective-permute-start | bytes 98312 | tf_op jit(solution)/shard_map/ppermute | solution.py:436
  14.7 4.3 %collective-permute-start.4 = (f32[16,512]{1,0:T(8,128)S(1)}, f32[16,512]{1,0:T(8,128)S(1)}, u32[]{:S(2)}, u32[]{:S(2)}) collective-permute-start(f32[16,512]{1,0:T(8,128)S(1)} %add_add_fusion), channel_id=1, source_target_pairs={{0,8},{4,12},{8,16},{12,20},{16,24},{20,28},{24,0},{28,4},{1,9},{5... | collective-permute-start | bytes 98312 | tf_op jit(solution)/shard_map/ppermute | solution.py:436
  19.1 27.1 %collective-permute-start.14 = (f32[4,2,8,64,128]{4,3,2,1,0:T(8,128)S(1)}, f32[4,2,8,64,128]{4,3,2,1,0:T(8,128)S(1)}, u32[]{:S(2)}, u32[]{:S(2)}) collective-permute-start(f32[4,2,8,64,128]{4,3,2,1,0:T(8,128)S(1)} %pad_maximum_fusion.refs_7_), channel_id=1, source_target_pairs={{0,8},{8,16},{16,24},{12,4},{20,12},{28,20},{1,9},{9,17},{17,25},{... | collective-permute-start | bytes 6291464 | tf_op jit(solution)/shard_map/ppermute | solution.py:423
  22.5 4.9 %collective-permute-start.9 = (f32[64,512]{1,0:T(8,128)S(1)}, f32[64,512]{1,0:T(8,128)S(1)}, u32[]{:S(2)}, u32[]{:S(2)}) collective-permute-start(f32[64,512]{1,0:T(8,128)S(1)} %pad_maximum_fusion.1.refs_1_), channel_id=1, source_target_pairs={{0,3},{1,2},{2,1},{3,0},{4,7},{5,6},{6,5},{7,4},{8,11},{9,10},{10,... | collective-permute-start | bytes 393224 | tf_op jit(solution)/shard_map/ppermute | solution.py:402
  22.6 6.1 %collective-permute-start.8 = (f32[64,512]{1,0:T(8,128)S(1)}, f32[64,512]{1,0:T(8,128)S(1)}, u32[]{:S(2)}, u32[]{:S(2)}) collective-permute-start(f32[64,512]{1,0:T(8,128)S(1)} %pad_maximum_fusion.1.refs_1_), channel_id=1, source_target_pairs={{0,2},{1,3},{2,0},{3,1},{4,6},{5,7},{6,4},{7,5},{8,10},{9,11},{10,... | collective-permute-start | bytes 393224 | tf_op jit(solution)/shard_map/ppermute | solution.py:402
  23.6 5.5 %collective-permute-start.7 = (f32[64,512]{1,0:T(8,128)S(1)}, f32[64,512]{1,0:T(8,128)S(1)}, u32[]{:S(2)}, u32[]{:S(2)}) collective-permute-start(f32[64,512]{1,0:T(8,128)S(1)} %pad_maximum_fusion.1.refs_1_), channel_id=1, source_target_pairs={{0,1},{1,0},{2,3},{3,2},{4,5},{5,4},{6,7},{7,6},{8,9},{9,8},{10,11... | collective-permute-start | bytes 393224 | tf_op jit(solution)/shard_map/ppermute | solution.py:402
  29.1 3.2 %collective-permute-start.10 = (f32[64,512]{1,0:T(8,128)S(1)}, f32[64,512]{1,0:T(8,128)S(1)}, u32[]{:S(2)}, u32[]{:S(2)}) collective-permute-start(f32[64,512]{1,0:T(8,128)S(1)} %pad_maximum_fusion.1.refs_1_), channel_id=1, source_target_pairs={{0,4},{4,0},{8,12},{12,8},{16,20},{20,16},{24,28},{28,24},{1,5},{5... | collective-permute-start | bytes 393224 | tf_op jit(solution)/shard_map/ppermute | solution.py:417
  31.4 1.7 %collective-permute-start.11 = (f32[64,512]{1,0:T(8,128)S(1)}, f32[64,512]{1,0:T(8,128)S(1)}, u32[]{:S(2)}, u32[]{:S(2)}) collective-permute-start(f32[64,512]{1,0:T(8,128)S(1)} %collective-permute-done.7.refs_2_), channel_id=1, source_target_pairs={{0,4},{4,0},{8,12},{12,8},{16,20},{20,16},{24,28},{28,24},{1,5},{5... | collective-permute-start | bytes 393224 | tf_op jit(solution)/shard_map/ppermute | solution.py:417
  31.4 1.7 %collective-permute-start.12 = (f32[64,512]{1,0:T(8,128)S(1)}, f32[64,512]{1,0:T(8,128)S(1)}, u32[]{:S(2)}, u32[]{:S(2)}) collective-permute-start(f32[64,512]{1,0:T(8,128)S(1)} %collective-permute-done.8.refs_3_), channel_id=1, source_target_pairs={{0,4},{4,0},{8,12},{12,8},{16,20},{20,16},{24,28},{28,24},{1,5},{5... | collective-permute-start | bytes 393224 | tf_op jit(solution)/shard_map/ppermute | solution.py:417
  31.9 1.3 %collective-permute-start.13 = (f32[64,512]{1,0:T(8,128)S(1)}, f32[64,512]{1,0:T(8,128)S(1)}, u32[]{:S(2)}, u32[]{:S(2)}) collective-permute-start(f32[64,512]{1,0:T(8,128)S(1)} %collective-permute-done.9.refs_4_), channel_id=1, source_target_pairs={{0,4},{4,0},{8,12},{12,8},{16,20},{20,16},{24,28},{28,24},{1,5},{5... | collective-permute-start | bytes 393224 | tf_op jit(solution)/shard_map/ppermute | solution.py:417
  32.3 10.0 %collective-permute-start.15 = (f32[200,512]{1,0:T(8,128)S(1)}, f32[200,512]{1,0:T(8,128)S(1)}, u32[]{:S(2)}, u32[]{:S(2)}) collective-permute-start(f32[200,512]{1,0:T(8,128)S(1)} %slice.35), channel_id=1, source_target_pairs={{0,1},{4,5},{8,9},{12,13},{16,17},{20,21},{24,25},{28,29}} | collective-permute-start | bytes 1228808 | tf_op jit(solution)/shard_map/ppermute | solution.py:418
  46.2 26.3 %collective-permute-start.20 = (f32[4,2,8,64,128]{4,3,2,1,0:T(8,128)S(1)}, f32[4,2,8,64,128]{4,3,2,1,0:T(8,128)S(1)}, u32[]{:S(2)}, u32[]{:S(2)}) collective-permute-start(f32[4,2,8,64,128]{4,3,2,1,0:T(8,128)S(1)} %collective-permute-done.14.refs_8_), channel_id=1, source_target_pairs={{8,16},{16,24},{12,4},{20,12},{9,17},{17,25},{13,5},{21,13},{10,18... | collective-permute-start | bytes 6291464 | tf_op jit(solution)/shard_map/ppermute | solution.py:423
  49.7 10.4 %collective-permute-start.16 = (f32[200,512]{1,0:T(8,128)S(1)}, f32[200,512]{1,0:T(8,128)S(1)}, u32[]{:S(2)}, u32[]{:S(2)}) collective-permute-start(f32[200,512]{1,0:T(8,128)S(1)} %slice_add_fusion.2.refs_3_), channel_id=1, source_target_pairs={{0,2},{1,3},{4,6},{5,7},{8,10},{9,11},{12,14},{13,15},{16,18},{17,... | collective-permute-start | bytes 1228808 | tf_op jit(solution)/shard_map/ppermute | solution.py:418
  51.1 8.1 %collective-permute-start.17 = (f32[152,512]{1,0:T(8,128)S(1)}, f32[152,512]{1,0:T(8,128)S(1)}, u32[]{:S(2)}, u32[]{:S(2)}) collective-permute-start(f32[152,512]{1,0:T(8,128)S(1)} %slice.36), channel_id=1, source_target_pairs={{0,1},{4,5},{8,9},{12,13},{16,17},{20,21},{24,25},{28,29}} | collective-permute-start | bytes 933896 | tf_op jit(solution)/shard_map/ppermute | solution.py:418
  51.8 16.1 %collective-permute-start.19 = (f32[160,512]{1,0:T(8,128)S(1)}, f32[160,512]{1,0:T(8,128)S(1)}, u32[]{:S(2)}, u32[]{:S(2)}) collective-permute-start(f32[160,512]{1,0:T(8,128)S(1)} %slice.37), channel_id=1, source_target_pairs={{0,1},{4,5},{8,9},{12,13},{16,17},{20,21},{24,25},{28,29}} | collective-permute-start | bytes 983048 | tf_op jit(solution)/shard_map/ppermute | solution.py:418
  52.5 44.8 %slice-start = ((s8[9437184]{0:T(1024)(128)(4,1)}), s8[4194304]{0:T(1024)(128)(4,1)S(1)}, s32[]{:S(2)}) async-start(s8[9437184]{0:T(1024)(128)(4,1)} %bitcast.12), calls=%async_computation | async-start | bytes 8388608
  60.2 8.9 %collective-permute-start.18 = (f32[152,512]{1,0:T(8,128)S(1)}, f32[152,512]{1,0:T(8,128)S(1)}, u32[]{:S(2)}, u32[]{:S(2)}) collective-permute-start(f32[152,512]{1,0:T(8,128)S(1)} %slice_add_fusion.refs_5_), channel_id=1, source_target_pairs={{0,2},{1,3},{4,6},{5,7},{8,10},{9,11},{12,14},{13,15},{16,18},{17,... | collective-permute-start | bytes 933896 | tf_op jit(solution)/shard_map/ppermute | solution.py:418
  61.7 35.6 %slice-start.1 = ((s8[9437184]{0:T(1024)(128)(4,1)}), s8[4194304]{0:T(1024)(128)(4,1)S(1)}, s32[]{:S(2)}) async-start(s8[9437184]{0:T(1024)(128)(4,1)} %bitcast.12), calls=%async_computation.1 | async-start | bytes 8388608
  72.7 21.0 %collective-permute-start.22 = (f32[2,2,8,64,128]{4,3,2,1,0:T(8,128)S(1)}, f32[2,2,8,64,128]{4,3,2,1,0:T(8,128)S(1)}, u32[]{:S(2)}, u32[]{:S(2)}) collective-permute-start(f32[2,2,8,64,128]{4,3,2,1,0:T(8,128)S(1)} %get-tuple-element.117), channel_id=1, source_target_pairs={{16,24},{12,4},{17,25},{13,5},{18,26},{14,6},{19,27},{15,7}} | collective-permute-start | bytes 3145736 | tf_op jit(solution)/shard_map/ppermute | solution.py:423
  73.4 23.8 %collective-permute-start.23 = (f32[4,2,8,64,128]{4,3,2,1,0:T(8,128)S(1)}, f32[4,2,8,64,128]{4,3,2,1,0:T(8,128)S(1)}, u32[]{:S(2)}, u32[]{:S(2)}) collective-permute-start(f32[4,2,8,64,128]{4,3,2,1,0:T(8,128)S(1)} %collective-permute-done.14.refs_8_), channel_id=1, source_target_pairs={{0,4},{4,0},{8,12},{12,8},{16,20},{20,16},{24,28},{28,24},{1,5},{5... | collective-permute-start | bytes 6291464 | tf_op jit(solution)/shard_map/ppermute | solution.py:417
  80.4 16.9 %collective-permute-start.24 = (f32[4,2,8,64,128]{4,3,2,1,0:T(8,128)S(1)}, f32[4,2,8,64,128]{4,3,2,1,0:T(8,128)S(1)}, u32[]{:S(2)}, u32[]{:S(2)}) collective-permute-start(f32[4,2,8,64,128]{4,3,2,1,0:T(8,128)S(1)} %collective-permute-done.20.refs_9_), channel_id=1, source_target_pairs={{0,4},{4,0},{8,12},{12,8},{16,20},{20,16},{24,28},{28,24},{1,5},{5... | collective-permute-start | bytes 6291464 | tf_op jit(solution)/shard_map/ppermute | solution.py:417
  80.5 10.7 %collective-permute-start.21 = (f32[160,512]{1,0:T(8,128)S(1)}, f32[160,512]{1,0:T(8,128)S(1)}, u32[]{:S(2)}, u32[]{:S(2)}) collective-permute-start(f32[160,512]{1,0:T(8,128)S(1)} %slice_add_fusion.1.refs_7_), channel_id=1, source_target_pairs={{0,2},{1,3},{4,6},{5,7},{8,10},{9,11},{12,14},{13,15},{16,18},{17,... | collective-permute-start | bytes 983048 | tf_op jit(solution)/shard_map/ppermute | solution.py:418
  81.8 15.5 %slice-start.2 = ((s8[9437184]{0:T(1024)(128)(4,1)}), s8[1048576]{0:T(1024)(128)(4,1)S(1)}, s32[]{:S(2)}) async-start(s8[9437184]{0:T(1024)(128)(4,1)} %bitcast.12), calls=%async_computation.2 | async-start | bytes 2097152
  93.7 3.6 %collective-permute-start.25 = (f32[2,2,8,64,128]{4,3,2,1,0:T(8,128)S(1)}, f32[2,2,8,64,128]{4,3,2,1,0:T(8,128)S(1)}, u32[]{:S(2)}, u32[]{:S(2)}) collective-permute-start(f32[2,2,8,64,128]{4,3,2,1,0:T(8,128)S(1)} %collective-permute-done.22.refs_10_), channel_id=1, source_target_pairs={{0,4},{4,0},{8,12},{12,8},{16,20},{20,16},{24,28},{28,24},{1,5},{5... | collective-permute-start | bytes 3145736 | tf_op jit(solution)/shard_map/ppermute | solution.py:417
  95.0 10.3 %collective-permute-start.26 = (f32[2,2,8,64,128]{4,3,2,1,0:T(8,128)S(1)}, f32[2,2,8,64,128]{4,3,2,1,0:T(8,128)S(1)}, u32[]{:S(2)}, u32[]{:S(2)}) collective-permute-start(f32[2,2,8,64,128]{4,3,2,1,0:T(8,128)S(1)} %get-tuple-element.116), channel_id=1, source_target_pairs={{16,24},{12,4},{17,25},{13,5},{18,26},{14,6},{19,27},{15,7}} | collective-permute-start | bytes 3145736 | tf_op jit(solution)/shard_map/ppermute | solution.py:423
  105.3 6.2 %collective-permute-start.27 = (f32[2,2,8,64,128]{4,3,2,1,0:T(8,128)S(1)}, f32[2,2,8,64,128]{4,3,2,1,0:T(8,128)S(1)}, u32[]{:S(2)}, u32[]{:S(2)}) collective-permute-start(f32[2,2,8,64,128]{4,3,2,1,0:T(8,128)S(1)} %collective-permute-done.26.refs_10_), channel_id=1, source_target_pairs={{0,4},{4,0},{8,12},{12,8},{16,20},{20,16},{24,28},{28,24},{1,5},{5... | collective-permute-start | bytes 3145736 | tf_op jit(solution)/shard_map/ppermute | solution.py:417
where the time goes:
time: 122 us; the launch traced here: 121 us
  Pallas kernels  52.6 us (43%)
  starting transfers between devices  39 us (32%)
  waiting for transfers between devices  26.2 us (21%)
  local copies, waits for them, and re-layouts  1.59 us (1%)
  between operations  1.25 us (1%)
    pallas_call x3, Pallas kernels, cholesky_next(): call(functools.partial(cholesky_kernel, first, last, 0, 0), [f32(*state[0...  18.8 us
    pallas_call x2, Pallas kernels, update(): call(functools.partial(update_kernel, chunks, [start for _, start in sour...  17.5 us
    ppermute x9, starting transfers between devices, body(): swap = lambda value: lax.ppermute(value, 'row', other_core)  15.8 us
    pallas_call x1, Pallas kernels, cholesky_start(): call(functools.partial(cholesky_kernel, 0, last, len(own), n_z), [f32(til...  9.12 us
    ppermute x4, starting transfers between devices, hop(): return lax.ppermute(value, 'row', pairs)  8.3 us
    ppermute x4, waiting for transfers between devices, hop(): return lax.ppermute(value, 'row', pairs)  7.29 us
    ppermute x6, starting transfers between devices, body(): lax.ppermute(value, 'col', [(i, i + level) for i in range(level)])  6.09 us
    ppermute x6, waiting for transfers between devices, body(): lax.ppermute(value, 'col', [(i, i + level) for i in range(level)])  5.63 us
  transfers between devices with their start and end apart: 28, of which 13 were waited for; matrix products, arithmetic and copies ran while one was open for 0% of the time, Pallas kernels for 35%

commit v1 on v0

--- a/solution.py
+++ b/solution.py
@@ -194,9 +194,9 @@
                     )
         for copy in copies:
             copy.start()
+        u_ref[...] = jnp.zeros_like(u_ref)
         for copy in copies:
             copy.wait()
-        u_ref[...] = jnp.zeros_like(u_ref)
     else:
         state_in, u_in, state, u_ref = refs
         state[...] = state_in[...]
@@ -445,7 +445,7 @@
     others = [swap(half) for half in halves]
 
     height = panel.shape[0]
-    bounds = [0, height * 2 // 5 // SUBLANES * SUBLANES, height * 7 // 10 // SUBLANES * SUBLANES, height]
+    bounds = [0, height * 2 // 5 // SUBLANES * SUBLANES, height * 3 // 4 // SUBLANES * SUBLANES, height]
     held = [panel[first:last] for first, last in zip(bounds[:-1], bounds[1:])]
     sent = [None] * len(held)
 

time: 122 us -> 122 us (level)
  waiting for transfers between devices: 26.2 us -> 24.7 us
  starting transfers between devices: 39 us -> 40.4 us
    ppermute x6, waiting for transfers between devices: 5.63 us -> 4.13 us  [body(): lax.ppermute(value, 'col', [(i, i + level) for i in range(level)])]
    ppermute x9, starting transfers between devices: 15.8 us -> 17.2 us  [body(): swap = lambda value: lax.ppermute(value, 'row', other_core)]
where the time goes in v1:
time: 122 us; the launch traced here: 121 us
  Pallas kernels  52.6 us (43%)
  starting transfers between devices  40.4 us (33%)
  waiting for transfers between devices  24.7 us (20%)
  local copies, waits for them, and re-layouts  1.64 us (1%)
  between operations  1.25 us (1%)
    pallas_call x3, Pallas kernels, cholesky_next(): call(functools.partial(cholesky_kernel, first, last, 0, 0), [f32(*state[0...  18.8 us
    pallas_call x2, Pallas kernels, update(): call(functools.partial(update_kernel, chunks, [start for _, start in sour...  17.5 us
    ppermute x9, starting transfers between devices, body(): swap = lambda value: lax.ppermute(value, 'row', other_core)  17.2 us
    pallas_call x1, Pallas kernels, cholesky_start(): call(functools.partial(cholesky_kernel, 0, last, len(own), n_z), [f32(til...  9.19 us
    ppermute x4, starting transfers between devices, hop(): return lax.ppermute(value, 'row', pairs)  8.3 us
    ppermute x4, waiting for transfers between devices, hop(): return lax.ppermute(value, 'row', pairs)  7.29 us
    ppermute x6, starting transfers between devices, body(): lax.ppermute(value, 'col', [(i, i + level) for i in range(level)])  6.09 us
    ppermute x3, waiting for transfers between devices, scatter(): lax.ppermute(part, axis, [(root, i)])  4.87 us
  transfers between devices with their start and end apart: 28, of which 13 were waited for; matrix products, arithmetic and copies ran while one was open for 0% of the time, Pallas kernels for 35%

profile of v1, /device:TPU:21, one launch (start us, length us, event | category | flops | bytes accessed | tf_op | source)
XLA Modules:
  0.0 121.3 jit_solution(13510224769981407113)
XLA Ops:
  0.6 1.3 %slice_bitcast_fusion.refs_0_ = f32[64,8,512]{2,1,0:T(8,128)S(1)} fusion(f32[9,64,8,512]{3,2,1,0:T(8,128)} %refs_1_.5), kind=kLoop, calls=%fused_computation.3 | loop fusion | bytes 2097152 | tf_op jit(solution)/shard_map/squeeze | solution.py:427
  4.6 1.3 %collective-permute-start.1 = (f32[16,512]{1,0:T(8,128)S(1)}, f32[16,512]{1,0:T(8,128)S(1)}, u32[]{:S(2)}, u32[]{:S(2)}) collective-permute-start(f32[16,512]{1,0:T(8,128)S(1)} %get-tuple-element.122), channel_id=1, source_target_pairs={{0,2},{4,6},{8,10},{12,14},{16,18},{20,22},{24,26},{28,30}} | collective-permute-start | bytes 98312 | tf_op jit(solution)/shard_map/ppermute | solution.py:397
  6.0 4.9 %collective-permute-done.1 = f32[16,512]{1,0:T(8,128)S(1)} collective-permute-done((f32[16,512]{1,0:T(8,128)S(1)}, f32[16,512]{1,0:T(8,128)S(1)}, u32[]{:S(2)}, u32[]{:S(2)}) %collective-permute-start.1) | collective-permute-done | bytes 32800 | tf_op jit(solution)/shard_map/ppermute | solution.py:397
  11.5 3.2 %collective-permute-start.5 = (f32[16,512]{1,0:T(8,128)S(1)}, f32[16,512]{1,0:T(8,128)S(1)}, u32[]{:S(2)}, u32[]{:S(2)}) collective-permute-start(f32[16,512]{1,0:T(8,128)S(1)} %add_add_fusion), channel_id=1, source_target_pairs={{0,16},{4,20},{8,24},{12,28},{16,0},{20,4},{24,8},{28,12},{1,17},{... | collective-permute-start | bytes 98312 | tf_op jit(solution)/shard_map/ppermute | solution.py:436
  14.8 4.2 %shard_map.31 = (f32[8,64,512]{2,1,0:T(8,128)S(1)}, f32[8,128]{1,0:T(8,128)S(1)}) custom-call(f32[8,128]{1,0:T(8,128)S(1)} %get-tuple-element.64._, s32[3]{0:T(128)S(1)} %pad_add_fusion.refs_0_, f32[9,64,8,512]{3,2,1,0:T(8,128)} %refs_1_.5), custom_call_target="tpu_custom_call" | custom-call | flops 200000000 | tf_op jit(solution)/shard_map/pallas_call | solution.py:89
  19.1 3.4 %collective-permute-start.14 = (f32[4,2,8,64,128]{4,3,2,1,0:T(8,128)S(1)}, f32[4,2,8,64,128]{4,3,2,1,0:T(8,128)S(1)}, u32[]{:S(2)}, u32[]{:S(2)}) collective-permute-start(f32[4,2,8,64,128]{4,3,2,1,0:T(8,128)S(1)} %pad_maximum_fusion.refs_7_), channel_id=1, source_target_pairs={{0,8},{8,16},{16,24},{12,4},{20,12},{28,20},{1,9},{9,17},{17,25},{... | collective-permute-start | bytes 6291464 | tf_op jit(solution)/shard_map/ppermute | solution.py:423
  22.6 1.1 collective-permute-start.8
  23.6 1.6 %collective-permute-start.7 = (f32[64,512]{1,0:T(8,128)S(1)}, f32[64,512]{1,0:T(8,128)S(1)}, u32[]{:S(2)}, u32[]{:S(2)}) collective-permute-start(f32[64,512]{1,0:T(8,128)S(1)} %pad_maximum_fusion.1.refs_1_), channel_id=1, source_target_pairs={{0,1},{1,0},{2,3},{3,2},{4,5},{5,4},{6,7},{7,6},{8,9},{9,8},{10,11... | collective-permute-start | bytes 393224 | tf_op jit(solution)/shard_map/ppermute | solution.py:402
  25.2 2.2 %collective-permute-done.9.refs_4_ = f32[64,512]{1,0:T(8,128)S(1)} collective-permute-done((f32[64,512]{1,0:T(8,128)S(1)}, f32[64,512]{1,0:T(8,128)S(1)}, u32[]{:S(2)}, u32[]{:S(2)}) %collective-permute-start.9) | collective-permute-done | bytes 131104 | tf_op jit(solution)/shard_map/ppermute | solution.py:402
  27.4 1.3 %collective-permute-done.8.refs_3_ = f32[64,512]{1,0:T(8,128)S(1)} collective-permute-done((f32[64,512]{1,0:T(8,128)S(1)}, f32[64,512]{1,0:T(8,128)S(1)}, u32[]{:S(2)}, u32[]{:S(2)}) %collective-permute-start.8) | collective-permute-done | bytes 131104 | tf_op jit(solution)/shard_map/ppermute | solution.py:402
  29.1 2.3 %collective-permute-start.10 = (f32[64,512]{1,0:T(8,128)S(1)}, f32[64,512]{1,0:T(8,128)S(1)}, u32[]{:S(2)}, u32[]{:S(2)}) collective-permute-start(f32[64,512]{1,0:T(8,128)S(1)} %pad_maximum_fusion.1.refs_1_), channel_id=1, source_target_pairs={{0,4},{4,0},{8,12},{12,8},{16,20},{20,16},{24,28},{28,24},{1,5},{5... | collective-permute-start | bytes 393224 | tf_op jit(solution)/shard_map/ppermute | solution.py:417
  33.2 9.2 %shard_map.32 = (f32[512,512]{1,0:T(8,128)S(1)}, f32[512,512]{1,0:T(8,128)S(1)}, f32[8,128]{1,0:T(8,128)S(1)}) custom-call(f32[8,128]{1,0:T(8,128)S(1)} %get-tuple-element.66._, s32[3]{0:T(128)S(1)} %pad_add_fusion.refs_0_, f32[64,512]{1,0:T(8,128)S(1)} %pad_maximum_fusion.1.refs_1_, f32[64,512]{1,0:T(8,128)S(1)} %collective-permute-done.7.refs_2_, ...), custom_call_target="tpu_custom_call" | custom-call | flops 3000000000 | tf_op jit(solution)/shard_map/pallas_call | solution.py:214
  42.4 3.8 %collective-permute-done.14.refs_8_ = f32[4,2,8,64,128]{4,3,2,1,0:T(8,128)S(1)} collective-permute-done((f32[4,2,8,64,128]{4,3,2,1,0:T(8,128)S(1)}, f32[4,2,8,64,128]{4,3,2,1,0:T(8,128)S(1)}, u32[]{:S(2)}, u32[]{:S(2)}) %collective-permute-start.14) | collective-permute-done | bytes 2097184 | tf_op jit(solution)/shard_map/ppermute | solution.py:423
  46.2 3.5 %collective-permute-start.20 = (f32[4,2,8,64,128]{4,3,2,1,0:T(8,128)S(1)}, f32[4,2,8,64,128]{4,3,2,1,0:T(8,128)S(1)}, u32[]{:S(2)}, u32[]{:S(2)}) collective-permute-start(f32[4,2,8,64,128]{4,3,2,1,0:T(8,128)S(1)} %collective-permute-done.14.refs_8_), channel_id=1, source_target_pairs={{8,16},{16,24},{12,4},{20,12},{9,17},{17,25},{13,5},{21,13},{10,18... | collective-permute-start | bytes 6291464 | tf_op jit(solution)/shard_map/ppermute | solution.py:423
  49.7 1.3 %collective-permute-start.16 = (f32[200,512]{1,0:T(8,128)S(1)}, f32[200,512]{1,0:T(8,128)S(1)}, u32[]{:S(2)}, u32[]{:S(2)}) collective-permute-start(f32[200,512]{1,0:T(8,128)S(1)} %slice_add_fusion.2.refs_3_), channel_id=1, source_target_pairs={{0,2},{1,3},{4,6},{5,7},{8,10},{9,11},{12,14},{13,15},{16,18},{17,... | collective-permute-start | bytes 1228808 | tf_op jit(solution)/shard_map/ppermute | solution.py:418
  51.8 6.7 %shard_map.33 = (f32[512,512]{1,0:T(8,128)S(1)}, f32[512,512]{1,0:T(8,128)S(1)}, f32[8,128]{1,0:T(8,128)S(1)}) custom-call(f32[8,128]{1,0:T(8,128)S(1)} %get-tuple-element.76._, s32[3]{0:T(128)S(1)} %pad_add_fusion.refs_0_, f32[512,512]{1,0:T(8,128)S(1)} %get-tuple-element.77.refs_1_, f32[512,512]{1,0:T(8,128)S(1)} %get-tuple-element.78.refs_2_), custom_call_target="tpu_custom_call" | custom-call | flops 1000000000 | tf_op jit(solution)/shard_map/pallas_call | solution.py:226
  58.5 1.6 %collective-permute-done.16.refs_4_ = f32[200,512]{1,0:T(8,128)S(1)} collective-permute-done((f32[200,512]{1,0:T(8,128)S(1)}, f32[200,512]{1,0:T(8,128)S(1)}, u32[]{:S(2)}, u32[]{:S(2)}) %collective-permute-start.16) | collective-permute-done | bytes 409632 | tf_op jit(solution)/shard_map/ppermute | solution.py:418
  60.2 1.3 %collective-permute-start.18 = (f32[184,512]{1,0:T(8,128)S(1)}, f32[184,512]{1,0:T(8,128)S(1)}, u32[]{:S(2)}, u32[]{:S(2)}) collective-permute-start(f32[184,512]{1,0:T(8,128)S(1)} %slice_add_fusion.1.refs_5_), channel_id=1, source_target_pairs={{0,2},{1,3},{4,6},{5,7},{8,10},{9,11},{12,14},{13,15},{16,18},{17,... | collective-permute-start | bytes 1130504 | tf_op jit(solution)/shard_map/ppermute | solution.py:418
  61.5 0.9 collective-permute-start.19
  62.4 6.3 %shard_map.34 = (f32[512,512]{1,0:T(8,128)S(1)}, f32[512,512]{1,0:T(8,128)S(1)}, f32[8,128]{1,0:T(8,128)S(1)}) custom-call(f32[8,128]{1,0:T(8,128)S(1)} %get-tuple-element.81._, s32[3]{0:T(128)S(1)} %pad_add_fusion.refs_0_, f32[512,512]{1,0:T(8,128)S(1)} %get-tuple-element.82.refs_1_, f32[512,512]{1,0:T(8,128)S(1)} %get-tuple-element.83.refs_2_), custom_call_target="tpu_custom_call" | custom-call | flops 1000000000 | tf_op jit(solution)/shard_map/pallas_call | solution.py:226
  69.0 3.5 %collective-permute-done.20.refs_9_ = f32[4,2,8,64,128]{4,3,2,1,0:T(8,128)S(1)} collective-permute-done((f32[4,2,8,64,128]{4,3,2,1,0:T(8,128)S(1)}, f32[4,2,8,64,128]{4,3,2,1,0:T(8,128)S(1)}, u32[]{:S(2)}, u32[]{:S(2)}) %collective-permute-start.20) | collective-permute-done | bytes 2097184 | tf_op jit(solution)/shard_map/ppermute | solution.py:423
  73.5 7.0 %collective-permute-start.23 = (f32[4,2,8,64,128]{4,3,2,1,0:T(8,128)S(1)}, f32[4,2,8,64,128]{4,3,2,1,0:T(8,128)S(1)}, u32[]{:S(2)}, u32[]{:S(2)}) collective-permute-start(f32[4,2,8,64,128]{4,3,2,1,0:T(8,128)S(1)} %collective-permute-done.14.refs_8_), channel_id=1, source_target_pairs={{0,4},{4,0},{8,12},{12,8},{16,20},{20,16},{24,28},{28,24},{1,5},{5... | collective-permute-start | bytes 6291464 | tf_op jit(solution)/shard_map/ppermute | solution.py:417
  80.6 1.3 %collective-permute-start.21 = (f32[128,512]{1,0:T(8,128)S(1)}, f32[128,512]{1,0:T(8,128)S(1)}, u32[]{:S(2)}, u32[]{:S(2)}) collective-permute-start(f32[128,512]{1,0:T(8,128)S(1)} %slice_add_fusion.refs_7_), channel_id=1, source_target_pairs={{0,2},{1,3},{4,6},{5,7},{8,10},{9,11},{12,14},{13,15},{16,18},{17,... | collective-permute-start | bytes 786440 | tf_op jit(solution)/shard_map/ppermute | solution.py:418
  81.9 5.8 %shard_map.35 = (f32[512,512]{1,0:T(8,128)S(1)}, f32[512,512]{1,0:T(8,128)S(1)}, f32[8,128]{1,0:T(8,128)S(1)}) custom-call(f32[8,128]{1,0:T(8,128)S(1)} %get-tuple-element.88._, s32[3]{0:T(128)S(1)} %pad_add_fusion.refs_0_, f32[512,512]{1,0:T(8,128)S(1)} %get-tuple-element.89.refs_1_, f32[512,512]{1,0:T(8,128)S(1)} %get-tuple-element.90.refs_2_), custom_call_target="tpu_custom_call" | custom-call | flops 1000000000 | tf_op jit(solution)/shard_map/pallas_call | solution.py:226
  87.7 2.2 %collective-permute-done.21.refs_8_ = f32[128,512]{1,0:T(8,128)S(1)} collective-permute-done((f32[128,512]{1,0:T(8,128)S(1)}, f32[128,512]{1,0:T(8,128)S(1)}, u32[]{:S(2)}, u32[]{:S(2)}) %collective-permute-start.21) | collective-permute-done | bytes 262176 | tf_op jit(solution)/shard_map/ppermute | solution.py:418
  89.9 2.4 %shard_map.36 = (bf16[512,512]{1,0:T(8,128)(2,1)S(1)}, bf16[512,512]{1,0:T(8,128)(2,1)S(1)}, bf16[512,512]{1,0:T(8,128)(2,1)S(1)}, bf16[512,512]{1,0:T(8,128)(2,...) custom-call(f32[8,128]{1,0:T(8,128)S(1)} %get-tuple-element.93._, s32[3]{0:T(128)S(1)} %pad_add_fusion.refs_0_, ...), custom_call_target="tpu_custom_call" | custom-call | flops 50000000 | tf_op jit(solution)/shard_map/pallas_call | solution.py:258
  92.3 1.3 %collective-permute-start.25 = (f32[2,2,8,64,128]{4,3,2,1,0:T(8,128)S(1)}, f32[2,2,8,64,128]{4,3,2,1,0:T(8,128)S(1)}, u32[]{:S(2)}, u32[]{:S(2)}) collective-permute-start(f32[2,2,8,64,128]{4,3,2,1,0:T(8,128)S(1)} %collective-permute-done.22.refs_10_), channel_id=1, source_target_pairs={{0,4},{4,0},{8,12},{12,8},{16,20},{20,16},{24,28},{28,24},{1,5},{5... | collective-permute-start | bytes 3145736 | tf_op jit(solution)/shard_map/ppermute | solution.py:417
  94.4 1.6 %collective-permute-done.25.refs_13_ = f32[2,2,8,64,128]{4,3,2,1,0:T(8,128)S(1)} collective-permute-done((f32[2,2,8,64,128]{4,3,2,1,0:T(8,128)S(1)}, f32[2,2,8,64,128]{4,3,2,1,0:T(8,128)S(1)}, u32[]{:S(2)}, u32[]{:S(2)}) %collective-permute-start.25) | collective-permute-done | bytes 1048608 | tf_op jit(solution)/shard_map/ppermute | solution.py:417
  96.0 8.0 %shard_map.37 = (f32[9,64,8,512]{3,2,1,0:T(8,128)}, f32[8,1,64,512]{3,2,1,0:T(8,128)}, f32[8,128]{1,0:T(8,128)S(1)}) custom-call(f32[8,128]{1,0:T(8,128)S(1)} %get-tuple-element.101._, s32[3]{0:T(128)S(1)} %pad_add_fusion.refs_0_, f32[9,64,8,512]{3,2,1,0:T(8,128)S(1)} %bitcast.13, bf16[512,512]{1,0:T(8,128)(2,1)S(1)} %get-tuple-element.102.refs_2_, ...), custom_call_target="tpu_custom_call" | custom-call | tf_op jit(solution)/shard_map/pallas_call | solution.py:382
  103.9 5.3 %collective-permute-start.27 = (f32[2,2,8,64,128]{4,3,2,1,0:T(8,128)S(1)}, f32[2,2,8,64,128]{4,3,2,1,0:T(8,128)S(1)}, u32[]{:S(2)}, u32[]{:S(2)}) collective-permute-start(f32[2,2,8,64,128]{4,3,2,1,0:T(8,128)S(1)} %collective-permute-done.26.refs_10_), channel_id=1, source_target_pairs={{0,4},{4,0},{8,12},{12,8},{16,20},{20,16},{24,28},{28,24},{1,5},{5... | collective-permute-start | bytes 3145736 | tf_op jit(solution)/shard_map/ppermute | solution.py:417
  109.3 2.3 %collective-permute-done.27.refs_13_ = f32[2,2,8,64,128]{4,3,2,1,0:T(8,128)S(1)} collective-permute-done((f32[2,2,8,64,128]{4,3,2,1,0:T(8,128)S(1)}, f32[2,2,8,64,128]{4,3,2,1,0:T(8,128)S(1)}, u32[]{:S(2)}, u32[]{:S(2)}) %collective-permute-start.27) | collective-permute-done | bytes 1048608 | tf_op jit(solution)/shard_map/ppermute | solution.py:417
  111.6 9.5 %shard_map.38 = (f32[9,64,8,512]{3,2,1,0:T(8,128)}, f32[8,1,64,512]{3,2,1,0:T(8,128)}, f32[8,128]{1,0:T(8,128)}) custom-call(f32[8,128]{1,0:T(8,128)S(1)} %get-tuple-element.110._, s32[3]{0:T(128)S(1)} %pad_add_fusion.refs_0_, f32[9,64,8,512]{3,2,1,0:T(8,128)S(1)} %bitcast.13, ...), custom_call_target="tpu_custom_call", output_to_operand_aliasing={{0}: (15, {}), {1}: (16, {})} | custom-call | tf_op jit(solution)/shard_map/pallas_call | solution.py:382
  (55 shorter events, 8.7 us)
Async XLA Ops:
  2.5 8.3 %collective-permute-start.3 = (f32[4,8,64,128]{3,2,1,0:T(8,128)S(1)}, f32[4,8,64,128]{3,2,1,0:T(8,128)S(1)}, u32[]{:S(2)}, u32[]{:S(2)}) collective-permute-start(f32[4,8,64,128]{3,2,1,0:T(8,128)S(1)} %get-tuple-element.60), channel_id=1, source_target_pairs={{0,4},{4,0},{8,12},{12,8},{16,20},{20,16},{24,28},{28,24},{1,5},{5... | collective-permute-start | bytes 3145736 | tf_op jit(solution)/shard_map/ppermute | solution.py:417
  3.3 2.7 %collective-permute-start = (f32[16,512]{1,0:T(8,128)S(1)}, f32[16,512]{1,0:T(8,128)S(1)}, u32[]{:S(2)}, u32[]{:S(2)}) collective-permute-start(f32[16,512]{1,0:T(8,128)S(1)} %get-tuple-element.120), channel_id=1, source_target_pairs={{0,1},{4,5},{8,9},{12,13},{16,17},{20,21},{24,25},{28,29}} | collective-permute-start | bytes 98312 | tf_op jit(solution)/shard_map/ppermute | solution.py:397
  3.9 2.0 %collective-permute-start.2 = (f32[16,512]{1,0:T(8,128)S(1)}, f32[16,512]{1,0:T(8,128)S(1)}, u32[]{:S(2)}, u32[]{:S(2)}) collective-permute-start(f32[16,512]{1,0:T(8,128)S(1)} %get-tuple-element.121), channel_id=1, source_target_pairs={{0,3},{4,7},{8,11},{12,15},{16,19},{20,23},{24,27},{28,31}} | collective-permute-start | bytes 98312 | tf_op jit(solution)/shard_map/ppermute | solution.py:397
  4.6 6.2 %collective-permute-start.1 = (f32[16,512]{1,0:T(8,128)S(1)}, f32[16,512]{1,0:T(8,128)S(1)}, u32[]{:S(2)}, u32[]{:S(2)}) collective-permute-start(f32[16,512]{1,0:T(8,128)S(1)} %get-tuple-element.122), channel_id=1, source_target_pairs={{0,2},{4,6},{8,10},{12,14},{16,18},{20,22},{24,26},{28,30}} | collective-permute-start | bytes 98312 | tf_op jit(solution)/shard_map/ppermute | solution.py:397
  11.3 7.8 %collective-permute-start.6 = (f32[16,512]{1,0:T(8,128)S(1)}, f32[16,512]{1,0:T(8,128)S(1)}, u32[]{:S(2)}, u32[]{:S(2)}) collective-permute-start(f32[16,512]{1,0:T(8,128)S(1)} %add_add_fusion), channel_id=1, source_target_pairs={{0,24},{4,28},{8,0},{12,4},{16,8},{20,12},{24,16},{28,20},{1,25},{... | collective-permute-start | bytes 98312 | tf_op jit(solution)/shard_map/ppermute | solution.py:436
  11.5 7.5 %collective-permute-start.5 = (f32[16,512]{1,0:T(8,128)S(1)}, f32[16,512]{1,0:T(8,128)S(1)}, u32[]{:S(2)}, u32[]{:S(2)}) collective-permute-start(f32[16,512]{1,0:T(8,128)S(1)} %add_add_fusion), channel_id=1, source_target_pairs={{0,16},{4,20},{8,24},{12,28},{16,0},{20,4},{24,8},{28,12},{1,17},{... | collective-permute-start | bytes 98312 | tf_op jit(solution)/shard_map/ppermute | solution.py:436
  14.7 4.3 %collective-permute-start.4 = (f32[16,512]{1,0:T(8,128)S(1)}, f32[16,512]{1,0:T(8,128)S(1)}, u32[]{:S(2)}, u32[]{:S(2)}) collective-permute-start(f32[16,512]{1,0:T(8,128)S(1)} %add_add_fusion), channel_id=1, source_target_pairs={{0,8},{4,12},{8,16},{12,20},{16,24},{20,28},{24,0},{28,4},{1,9},{5... | collective-permute-start | bytes 98312 | tf_op jit(solution)/shard_map/ppermute | solution.py:436
  19.1 27.1 %collective-permute-start.14 = (f32[4,2,8,64,128]{4,3,2,1,0:T(8,128)S(1)}, f32[4,2,8,64,128]{4,3,2,1,0:T(8,128)S(1)}, u32[]{:S(2)}, u32[]{:S(2)}) collective-permute-start(f32[4,2,8,64,128]{4,3,2,1,0:T(8,128)S(1)} %pad_maximum_fusion.refs_7_), channel_id=1, source_target_pairs={{0,8},{8,16},{16,24},{12,4},{20,12},{28,20},{1,9},{9,17},{17,25},{... | collective-permute-start | bytes 6291464 | tf_op jit(solution)/shard_map/ppermute | solution.py:423
  22.5 4.9 %collective-permute-start.9 = (f32[64,512]{1,0:T(8,128)S(1)}, f32[64,512]{1,0:T(8,128)S(1)}, u32[]{:S(2)}, u32[]{:S(2)}) collective-permute-start(f32[64,512]{1,0:T(8,128)S(1)} %pad_maximum_fusion.1.refs_1_), channel_id=1, source_target_pairs={{0,3},{1,2},{2,1},{3,0},{4,7},{5,6},{6,5},{7,4},{8,11},{9,10},{10,... | collective-permute-start | bytes 393224 | tf_op jit(solution)/shard_map/ppermute | solution.py:402
  22.6 6.1 %collective-permute-start.8 = (f32[64,512]{1,0:T(8,128)S(1)}, f32[64,512]{1,0:T(8,128)S(1)}, u32[]{:S(2)}, u32[]{:S(2)}) collective-permute-start(f32[64,512]{1,0:T(8,128)S(1)} %pad_maximum_fusion.1.refs_1_), channel_id=1, source_target_pairs={{0,2},{1,3},{2,0},{3,1},{4,6},{5,7},{6,4},{7,5},{8,10},{9,11},{10,... | collective-permute-start | bytes 393224 | tf_op jit(solution)/shard_map/ppermute | solution.py:402
  23.6 5.5 %collective-permute-start.7 = (f32[64,512]{1,0:T(8,128)S(1)}, f32[64,512]{1,0:T(8,128)S(1)}, u32[]{:S(2)}, u32[]{:S(2)}) collective-permute-start(f32[64,512]{1,0:T(8,128)S(1)} %pad_maximum_fusion.1.refs_1_), channel_id=1, source_target_pairs={{0,1},{1,0},{2,3},{3,2},{4,5},{5,4},{6,7},{7,6},{8,9},{9,8},{10,11... | collective-permute-start | bytes 393224 | tf_op jit(solution)/shard_map/ppermute | solution.py:402
  29.1 3.2 %collective-permute-start.10 = (f32[64,512]{1,0:T(8,128)S(1)}, f32[64,512]{1,0:T(8,128)S(1)}, u32[]{:S(2)}, u32[]{:S(2)}) collective-permute-start(f32[64,512]{1,0:T(8,128)S(1)} %pad_maximum_fusion.1.refs_1_), channel_id=1, source_target_pairs={{0,4},{4,0},{8,12},{12,8},{16,20},{20,16},{24,28},{28,24},{1,5},{5... | collective-permute-start | bytes 393224 | tf_op jit(solution)/shard_map/ppermute | solution.py:417
  31.4 1.7 %collective-permute-start.11 = (f32[64,512]{1,0:T(8,128)S(1)}, f32[64,512]{1,0:T(8,128)S(1)}, u32[]{:S(2)}, u32[]{:S(2)}) collective-permute-start(f32[64,512]{1,0:T(8,128)S(1)} %collective-permute-done.7.refs_2_), channel_id=1, source_target_pairs={{0,4},{4,0},{8,12},{12,8},{16,20},{20,16},{24,28},{28,24},{1,5},{5... | collective-permute-start | bytes 393224 | tf_op jit(solution)/shard_map/ppermute | solution.py:417
  31.4 1.7 %collective-permute-start.12 = (f32[64,512]{1,0:T(8,128)S(1)}, f32[64,512]{1,0:T(8,128)S(1)}, u32[]{:S(2)}, u32[]{:S(2)}) collective-permute-start(f32[64,512]{1,0:T(8,128)S(1)} %collective-permute-done.8.refs_3_), channel_id=1, source_target_pairs={{0,4},{4,0},{8,12},{12,8},{16,20},{20,16},{24,28},{28,24},{1,5},{5... | collective-permute-start | bytes 393224 | tf_op jit(solution)/shard_map/ppermute | solution.py:417
  31.9 1.3 %collective-permute-start.13 = (f32[64,512]{1,0:T(8,128)S(1)}, f32[64,512]{1,0:T(8,128)S(1)}, u32[]{:S(2)}, u32[]{:S(2)}) collective-permute-start(f32[64,512]{1,0:T(8,128)S(1)} %collective-permute-done.9.refs_4_), channel_id=1, source_target_pairs={{0,4},{4,0},{8,12},{12,8},{16,20},{20,16},{24,28},{28,24},{1,5},{5... | collective-permute-start | bytes 393224 | tf_op jit(solution)/shard_map/ppermute | solution.py:417
  32.3 10.1 %collective-permute-start.15 = (f32[200,512]{1,0:T(8,128)S(1)}, f32[200,512]{1,0:T(8,128)S(1)}, u32[]{:S(2)}, u32[]{:S(2)}) collective-permute-start(f32[200,512]{1,0:T(8,128)S(1)} %slice.35), channel_id=1, source_target_pairs={{0,1},{4,5},{8,9},{12,13},{16,17},{20,21},{24,25},{28,29}} | collective-permute-start | bytes 1228808 | tf_op jit(solution)/shard_map/ppermute | solution.py:418
  46.2 26.3 %collective-permute-start.20 = (f32[4,2,8,64,128]{4,3,2,1,0:T(8,128)S(1)}, f32[4,2,8,64,128]{4,3,2,1,0:T(8,128)S(1)}, u32[]{:S(2)}, u32[]{:S(2)}) collective-permute-start(f32[4,2,8,64,128]{4,3,2,1,0:T(8,128)S(1)} %collective-permute-done.14.refs_8_), channel_id=1, source_target_pairs={{8,16},{16,24},{12,4},{20,12},{9,17},{17,25},{13,5},{21,13},{10,18... | collective-permute-start | bytes 6291464 | tf_op jit(solution)/shard_map/ppermute | solution.py:423
  49.7 10.4 %collective-permute-start.16 = (f32[200,512]{1,0:T(8,128)S(1)}, f32[200,512]{1,0:T(8,128)S(1)}, u32[]{:S(2)}, u32[]{:S(2)}) collective-permute-start(f32[200,512]{1,0:T(8,128)S(1)} %slice_add_fusion.2.refs_3_), channel_id=1, source_target_pairs={{0,2},{1,3},{4,6},{5,7},{8,10},{9,11},{12,14},{13,15},{16,18},{17,... | collective-permute-start | bytes 1228808 | tf_op jit(solution)/shard_map/ppermute | solution.py:418
  51.1 7.4 %collective-permute-start.17 = (f32[184,512]{1,0:T(8,128)S(1)}, f32[184,512]{1,0:T(8,128)S(1)}, u32[]{:S(2)}, u32[]{:S(2)}) collective-permute-start(f32[184,512]{1,0:T(8,128)S(1)} %slice.36), channel_id=1, source_target_pairs={{0,1},{4,5},{8,9},{12,13},{16,17},{20,21},{24,25},{28,29}} | collective-permute-start | bytes 1130504 | tf_op jit(solution)/shard_map/ppermute | solution.py:418
  51.8 44.2 %slice-start = ((s8[9437184]{0:T(1024)(128)(4,1)}), s8[4194304]{0:T(1024)(128)(4,1)S(1)}, s32[]{:S(2)}) async-start(s8[9437184]{0:T(1024)(128)(4,1)} %bitcast.12), calls=%async_computation | async-start | bytes 8388608
  60.2 8.8 %collective-permute-start.18 = (f32[184,512]{1,0:T(8,128)S(1)}, f32[184,512]{1,0:T(8,128)S(1)}, u32[]{:S(2)}, u32[]{:S(2)}) collective-permute-start(f32[184,512]{1,0:T(8,128)S(1)} %slice_add_fusion.1.refs_5_), channel_id=1, source_target_pairs={{0,2},{1,3},{4,6},{5,7},{8,10},{9,11},{12,14},{13,15},{16,18},{17,... | collective-permute-start | bytes 1130504 | tf_op jit(solution)/shard_map/ppermute | solution.py:418
  61.5 7.1 %collective-permute-start.19 = (f32[128,512]{1,0:T(8,128)S(1)}, f32[128,512]{1,0:T(8,128)S(1)}, u32[]{:S(2)}, u32[]{:S(2)}) collective-permute-start(f32[128,512]{1,0:T(8,128)S(1)} %slice.37), channel_id=1, source_target_pairs={{0,1},{4,5},{8,9},{12,13},{16,17},{20,21},{24,25},{28,29}} | collective-permute-start | bytes 786440 | tf_op jit(solution)/shard_map/ppermute | solution.py:418
  62.4 33.5 %slice-start.1 = ((s8[9437184]{0:T(1024)(128)(4,1)}), s8[4194304]{0:T(1024)(128)(4,1)S(1)}, s32[]{:S(2)}) async-start(s8[9437184]{0:T(1024)(128)(4,1)} %bitcast.12), calls=%async_computation.1 | async-start | bytes 8388608
  72.8 19.5 %collective-permute-start.22 = (f32[2,2,8,64,128]{4,3,2,1,0:T(8,128)S(1)}, f32[2,2,8,64,128]{4,3,2,1,0:T(8,128)S(1)}, u32[]{:S(2)}, u32[]{:S(2)}) collective-permute-start(f32[2,2,8,64,128]{4,3,2,1,0:T(8,128)S(1)} %get-tuple-element.117), channel_id=1, source_target_pairs={{16,24},{12,4},{17,25},{13,5},{18,26},{14,6},{19,27},{15,7}} | collective-permute-start | bytes 3145736 | tf_op jit(solution)/shard_map/ppermute | solution.py:423
  73.5 22.4 %collective-permute-start.23 = (f32[4,2,8,64,128]{4,3,2,1,0:T(8,128)S(1)}, f32[4,2,8,64,128]{4,3,2,1,0:T(8,128)S(1)}, u32[]{:S(2)}, u32[]{:S(2)}) collective-permute-start(f32[4,2,8,64,128]{4,3,2,1,0:T(8,128)S(1)} %collective-permute-done.14.refs_8_), channel_id=1, source_target_pairs={{0,4},{4,0},{8,12},{12,8},{16,20},{20,16},{24,28},{28,24},{1,5},{5... | collective-permute-start | bytes 6291464 | tf_op jit(solution)/shard_map/ppermute | solution.py:417
  80.4 15.5 %collective-permute-start.24 = (f32[4,2,8,64,128]{4,3,2,1,0:T(8,128)S(1)}, f32[4,2,8,64,128]{4,3,2,1,0:T(8,128)S(1)}, u32[]{:S(2)}, u32[]{:S(2)}) collective-permute-start(f32[4,2,8,64,128]{4,3,2,1,0:T(8,128)S(1)} %collective-permute-done.20.refs_9_), channel_id=1, source_target_pairs={{0,4},{4,0},{8,12},{12,8},{16,20},{20,16},{24,28},{28,24},{1,5},{5... | collective-permute-start | bytes 6291464 | tf_op jit(solution)/shard_map/ppermute | solution.py:417
  80.6 9.3 %collective-permute-start.21 = (f32[128,512]{1,0:T(8,128)S(1)}, f32[128,512]{1,0:T(8,128)S(1)}, u32[]{:S(2)}, u32[]{:S(2)}) collective-permute-start(f32[128,512]{1,0:T(8,128)S(1)} %slice_add_fusion.refs_7_), channel_id=1, source_target_pairs={{0,2},{1,3},{4,6},{5,7},{8,10},{9,11},{12,14},{13,15},{16,18},{17,... | collective-permute-start | bytes 786440 | tf_op jit(solution)/shard_map/ppermute | solution.py:418
  81.9 14.1 %slice-start.2 = ((s8[9437184]{0:T(1024)(128)(4,1)}), s8[1048576]{0:T(1024)(128)(4,1)S(1)}, s32[]{:S(2)}) async-start(s8[9437184]{0:T(1024)(128)(4,1)} %bitcast.12), calls=%async_computation.2 | async-start | bytes 2097152
  92.3 3.6 %collective-permute-start.25 = (f32[2,2,8,64,128]{4,3,2,1,0:T(8,128)S(1)}, f32[2,2,8,64,128]{4,3,2,1,0:T(8,128)S(1)}, u32[]{:S(2)}, u32[]{:S(2)}) collective-permute-start(f32[2,2,8,64,128]{4,3,2,1,0:T(8,128)S(1)} %collective-permute-done.22.refs_10_), channel_id=1, source_target_pairs={{0,4},{4,0},{8,12},{12,8},{16,20},{20,16},{24,28},{28,24},{1,5},{5... | collective-permute-start | bytes 3145736 | tf_op jit(solution)/shard_map/ppermute | solution.py:417
  93.6 10.3 %collective-permute-start.26 = (f32[2,2,8,64,128]{4,3,2,1,0:T(8,128)S(1)}, f32[2,2,8,64,128]{4,3,2,1,0:T(8,128)S(1)}, u32[]{:S(2)}, u32[]{:S(2)}) collective-permute-start(f32[2,2,8,64,128]{4,3,2,1,0:T(8,128)S(1)} %get-tuple-element.116), channel_id=1, source_target_pairs={{16,24},{12,4},{17,25},{13,5},{18,26},{14,6},{19,27},{15,7}} | collective-permute-start | bytes 3145736 | tf_op jit(solution)/shard_map/ppermute | solution.py:423
  103.9 7.6 %collective-permute-start.27 = (f32[2,2,8,64,128]{4,3,2,1,0:T(8,128)S(1)}, f32[2,2,8,64,128]{4,3,2,1,0:T(8,128)S(1)}, u32[]{:S(2)}, u32[]{:S(2)}) collective-permute-start(f32[2,2,8,64,128]{4,3,2,1,0:T(8,128)S(1)} %collective-permute-done.26.refs_10_), channel_id=1, source_target_pairs={{0,4},{4,0},{8,12},{12,8},{16,20},{20,16},{24,28},{28,24},{1,5},{5... | collective-permute-start | bytes 3145736 | tf_op jit(solution)/shard_map/ppermute | solution.py:417
